TPU v7x, 32 devices: a whole 2x2x4 slice. The times are simulated.
32 devices in a mesh: grp: 2 (over x), row: 16 (over z, y, core).
Axes of the slice: x: 2, y: 2, z: 4, core: 2. Of those that a mesh axis runs over, the one named last changes fastest.
Arguments:
- matrix: bfloat16 [32, 2048, 16384], P(('grp', 'row')), parts along dimension 0, may hold values from -1 to 1
- probes: bfloat16 [16384, 128], P(('grp', 'row')), parts along dimension 0, may hold values from -6 to 6
Outputs:
- basis_out: bfloat16 [16384, 128], P(('grp', 'row')), parts along dimension 0
- sketch_out: bfloat16 [32, 4096, 128], P(('grp', 'row')), parts along dimension 0
There are 2 independent parts, one for each index of `grp`. A program takes and returns all parts, laid end to end along the dimension named above; each array names one. Nothing has to cross between parts.
All inputs are finite; a program needn't handle non-finite values.
Results may differ from a plain program's by a relative error of at most 0.012.
Values may be sent and summed in bfloat16 or wider, within the bound.
A program may use at most 192 MiB of HBM per device.

v0:
```python
import math
import jax
import jax.numpy as jnp
from jax import lax
from jax.sharding import PartitionSpec as P

GRID_ROWS = 4
ITERS = 2


def from_partner(shard, axis, bit):
    return lax.ppermute(shard, axis, [(i, i ^ 1 << bit) for i in range(lax.axis_size(axis))])


def orthonormal(product, gram_matrix, rescale):
    factor = jnp.linalg.cholesky(gram_matrix)
    solved = lax.linalg.triangular_solve(
        factor, product, left_side=False, lower=True, transpose_a=True
    )
    return (solved * rescale).astype(jnp.bfloat16)


def digit_set(device, level):
    return device // 2**level % 2 == 1


def per_device(matrix, probes):
    tile_block = matrix[0]
    tile_rows = tile_block.shape[0]
    grid_cols = lax.axis_size("row") // GRID_ROWS
    col_levels = grid_cols.bit_length() - 1
    row_levels = GRID_ROWS.bit_length() - 1
    device = lax.axis_index("row")
    rescale = math.sqrt(GRID_ROWS * tile_rows)
    current = probes
    sketch_block = None
    for iteration in range(ITERS):
        panel = current
        for level in range(col_levels):
            other = from_partner(panel, "row", level)
            panel = jnp.where(
                digit_set(device, level),
                jnp.concatenate([other, panel], 0),
                jnp.concatenate([panel, other], 0),
            )
        partial_value = lax.dot_general(
            tile_block, panel, (((0,), (0,)), ((), ())), preferred_element_type=jnp.float32
        )
        for level in range(row_levels):
            partial_value = partial_value + from_partner(
                partial_value.astype(jnp.bfloat16), "row", col_levels + level
            ).astype(partial_value.dtype)
        sketch = partial_value.astype(jnp.bfloat16)
        share_rows = sketch.shape[0] // GRID_ROWS
        grid_row = device // grid_cols
        sketch_block = lax.dynamic_slice_in_dim(sketch, grid_row * share_rows, share_rows, 0)
        image = jnp.dot(tile_block, sketch, preferred_element_type=jnp.float32)
        for level in reversed(range(col_levels)):
            half_rows = image.shape[0] // 2
            lower_part = image[:half_rows]
            upper_part = image[half_rows:]
            upward = digit_set(device, level)
            sent = jnp.where(upward, lower_part, upper_part)
            kept = jnp.where(upward, upper_part, lower_part)
            image = kept + from_partner(sent.astype(jnp.bfloat16), "row", level).astype(sent.dtype)
        local_gram = jnp.dot(
            image.T, image, precision=lax.Precision.HIGHEST, preferred_element_type=jnp.float32
        )
        gram_matrix = lax.psum(local_gram, "row")
        current = orthonormal(image, gram_matrix, rescale)
    return (current, sketch_block[None])


def solution(mesh):
    placed = (P(("grp", "row"), None, None), P(("grp", "row"), None))
    return jax.shard_map(
        per_device,
        mesh=mesh,
        in_specs=placed,
        out_specs=(P(("grp", "row"), None), P(("grp", "row"), None, None)),
        check_vma=False,
    )
```

profile of v0, /device:TPU:8, one launch (start us, length us, event | category | flops | bytes accessed | tf_op | source)
XLA Modules:
  0.0 968.9 jit_solution(17788045940890955766)
XLA Ops:
  7.2 1.0 copy.12
  8.3 1.3 collective-permute-done
  9.7 1.6 collective-permute-start.1
  11.3 6.8 collective-permute-done.1
  18.2 28.6 %fusion.50 = (bf16[16384,128]{0,1:T(8,128)(2,1)}, f32[16384,128]{0,1:T(8,128)}) fusion(bf16[1,2048,16384]{2,1,0:T(8,128)(2,1)} %param.5, bf16[1024,128]{0,1:T(8,128)(2,1)S(1)} %maximum_select_fusion.4, bf16[1024,128]{0,1:T(8,128)(2,1)S(1)} %collective-permute-done.1, pred[]{:T(512)S(6)} %eq.22), kind=kOutput, calls=%fused_computation.70 | convolution fusion | flops 8594391040 | bytes 80216064 | tf_op jit(solution)/shard_map/dot_general | solution.py:46
  46.7 0.2 collective-permute-start.2
  47.0 91.8 %collective-permute-done.2 = bf16[16384,128]{0,1:T(8,128)(2,1)S(1)} collective-permute-done((bf16[16384,128]{0,1:T(8,128)(2,1)}, bf16[16384,128]{0,1:T(8,128)(2,1)S(1)}, u32[]{:S(2)}, u32[]{:S(2)}) %collective-permute-start.2) | collective-permute-done | bytes 4194336 | tf_op jit(solution)/shard_map/ppermute | solution.py:12
  138.8 5.7 fusion.14
  144.5 2.7 collective-permute-start.3
  147.1 178.2 %collective-permute-done.3 = bf16[16384,128]{0,1:T(8,128)(2,1)} collective-permute-done((bf16[16384,128]{0,1:T(8,128)(2,1)S(1)}, bf16[16384,128]{0,1:T(8,128)(2,1)}, u32[]{:S(2)}, u32[]{:S(2)}) %collective-permute-start.3) | collective-permute-done | bytes 4194336 | tf_op jit(solution)/shard_map/ppermute | solution.py:12
  325.3 33.8 %fusion.16 = f32[2048,128]{0,1:T(8,128)S(1)} fusion(bf16[1,2048,16384]{2,1,0:T(8,128)(2,1)} %param.5, bf16[16384,128]{0,1:T(8,128)(2,1)} %collective-permute-done.3, f32[16384,128]{0,1:T(8,128)} %get-tuple-element.9, bf16[16384,128]{0,1:T(8,128)(2,1)} %copy-done), kind=kOutput, calls=%fused_computation.16 | convolution fusion | flops 8600420352 | bytes 84934656 | tf_op jit(solution)/shard_map/dot_general | solution.py:57
  359.2 1.6 collective-permute-start.4
  360.8 6.7 collective-permute-done.4
  367.7 1.3 collective-permute-done.5
  369.0 1.0 fusion.46
  370.3 89.0 %all-reduce.3.cloned.1.call-done = f32[128,128]{0,1:T(8,128)} async-done(((f32[128,128]{0,1:T(8,128)}), f32[128,128]{0,1:T(8,128)}) %all-reduce.3.cloned.1.call-update) | async-done | bytes 65552 | tf_op jit(solution)/shard_map/psum | solution.py:69
  459.3 0.9 copy.16
  460.3 0.9 fusion.43
  461.1 11.7 %cholesky.44 = f32[128,128]{1,0:T(8,128)S(1)} custom-call(f32[128,128]{1,0:T(8,128)S(1)} %fusion.43), custom_call_target="Cholesky" | custom-call | tf_op jit(solution)/shard_map/jit(cholesky)/cholesky | solution.py:16
  472.9 0.6 compare_reduce_fusion.1
  473.5 0.7 fusion.38
  474.2 9.8 %custom-call.6 = f32[1,128,128]{1,2,0:T(8,128)S(1)} custom-call(f32[1,128,128]{2,1,0:T(8,128)S(1)} %fusion.38), custom_call_target="InvertDiagBlocksLowerTriangular" | custom-call | tf_op jit(solution)/shard_map/triangular_solve/custom-call.0 | solution.py:17
  484.0 0.4 fusion.24
  484.5 1.3 collective-permute-done.6
  485.9 0.6 collective-permute-start.7
  486.6 7.8 collective-permute-done.7
  494.4 28.6 %fusion.51 = (bf16[16384,128]{0,1:T(8,128)(2,1)}, f32[16384,128]{0,1:T(8,128)}) fusion(bf16[1,2048,16384]{2,1,0:T(8,128)(2,1)} %param.5, bf16[1024,128]{0,1:T(8,128)(2,1)S(1)} %maximum_select_fusion.5, bf16[1024,128]{0,1:T(8,128)(2,1)S(1)} %collective-permute-done.7, pred[]{:T(512)S(6)} %eq.22), kind=kOutput, calls=%fused_computation.71 | convolution fusion | flops 8594391040 | bytes 80216064 | tf_op jit(solution)/shard_map/dot_general | solution.py:46
  523.0 92.0 %collective-permute-done.8 = bf16[16384,128]{0,1:T(8,128)(2,1)S(1)} collective-permute-done((bf16[16384,128]{0,1:T(8,128)(2,1)}, bf16[16384,128]{0,1:T(8,128)(2,1)S(1)}, u32[]{:S(2)}, u32[]{:S(2)}) %collective-permute-start.8) | collective-permute-done | bytes 4194336 | tf_op jit(solution)/shard_map/ppermute | solution.py:12
  615.0 4.4 fusion.15
  619.4 1.5 collective-permute-start.9
  620.9 178.3 %collective-permute-done.9 = bf16[16384,128]{0,1:T(8,128)(2,1)} collective-permute-done((bf16[16384,128]{0,1:T(8,128)(2,1)S(1)}, bf16[16384,128]{0,1:T(8,128)(2,1)}, u32[]{:S(2)}, u32[]{:S(2)}) %collective-permute-start.9) | collective-permute-done | bytes 4194336 | tf_op jit(solution)/shard_map/ppermute | solution.py:12
  799.2 8.2 add_convert_fusion
  807.4 29.7 %fusion.19 = f32[2048,128]{0,1:T(8,128)S(1)} fusion(bf16[16384,128]{0,1:T(8,128)(2,1)} %add_convert_fusion, bf16[1,2048,16384]{2,1,0:T(8,128)(2,1)} %param.5), kind=kOutput, calls=%fused_computation.17 | convolution fusion | flops 8589934592 | bytes 72351744 | tf_op jit(solution)/shard_map/dot_general | solution.py:57
  837.1 0.5 collective-permute-start.10
  837.6 7.8 collective-permute-done.10
  845.6 1.3 collective-permute-done.11
  846.9 1.0 fusion.47
  848.0 1.3 constant_dynamic-slice_fusion
  849.3 1.3 copy.19
  850.6 85.7 %all-reduce.5.cloned.1.call-done = f32[128,128]{0,1:T(8,128)} async-done(((f32[128,128]{0,1:T(8,128)}), f32[128,128]{0,1:T(8,128)}) %all-reduce.5.cloned.1.call-update) | async-done | bytes 65552 | tf_op jit(solution)/shard_map/psum | solution.py:69
  936.3 0.9 copy.18
  937.2 0.9 fusion.41
  938.0 11.7 %cholesky.55 = f32[128,128]{1,0:T(8,128)S(1)} custom-call(f32[128,128]{1,0:T(8,128)S(1)} %fusion.41), custom_call_target="Cholesky" | custom-call | tf_op jit(solution)/shard_map/jit(cholesky)/cholesky | solution.py:16
  949.8 0.6 compare_reduce_fusion
  950.4 0.7 fusion.39
  951.1 9.8 %custom-call.7 = f32[1,128,128]{1,2,0:T(8,128)S(1)} custom-call(f32[1,128,128]{2,1,0:T(8,128)S(1)} %fusion.39), custom_call_target="InvertDiagBlocksLowerTriangular" | custom-call | tf_op jit(solution)/shard_map/triangular_solve/custom-call.0 | solution.py:17
  960.9 0.4 fusion.25
  961.3 0.8 copy.20
  (21 shorter events, 1.2 us)
Async XLA Ops:
  7.2 452.2 %all-reduce.3.cloned.1.call-start = ((), (), s32[]{:S(2)}) async-start(), calls=%async_computation | async-start | bytes 131072 | tf_op jit(solution)/shard_map/psum | solution.py:69
  8.2 1.4 collective-permute-start
  9.7 8.4 collective-permute-start.1
  46.7 92.0 %collective-permute-start.2 = (bf16[16384,128]{0,1:T(8,128)(2,1)}, bf16[16384,128]{0,1:T(8,128)(2,1)S(1)}, u32[]{:S(2)}, u32[]{:S(2)}) collective-permute-start(bf16[16384,128]{0,1:T(8,128)(2,1)} %get-tuple-element.8), channel_id=1, source_target_pairs={{0,4},{1,5},{2,6},{3,7},{4,0},{5,1},{6,2},{7,3},{8,12},{9,13},{10,... | collective-permute-start | bytes 12582920 | tf_op jit(solution)/shard_map/ppermute | solution.py:12
  138.8 5.7 copy-start
  144.5 180.8 %collective-permute-start.3 = (bf16[16384,128]{0,1:T(8,128)(2,1)S(1)}, bf16[16384,128]{0,1:T(8,128)(2,1)}, u32[]{:S(2)}, u32[]{:S(2)}) collective-permute-start(bf16[16384,128]{0,1:T(8,128)(2,1)S(1)} %fusion.14), channel_id=1, source_target_pairs={{0,8},{1,9},{2,10},{3,11},{4,12},{5,13},{6,14},{7,15},{8,0},{9,1},... | collective-permute-start | bytes 12582920 | tf_op jit(solution)/shard_map/ppermute | solution.py:12
  359.2 8.3 collective-permute-start.4
  367.6 1.4 collective-permute-start.5
  370.1 566.2 %all-reduce.5.cloned.1.call-start = ((), (), s32[]{:S(2)}) async-start(), calls=%async_computation.1 | async-start | bytes 131072 | tf_op jit(solution)/shard_map/psum | solution.py:69
  484.4 1.4 collective-permute-start.6
  485.9 8.4 collective-permute-start.7
  523.0 92.0 %collective-permute-start.8 = (bf16[16384,128]{0,1:T(8,128)(2,1)}, bf16[16384,128]{0,1:T(8,128)(2,1)S(1)}, u32[]{:S(2)}, u32[]{:S(2)}) collective-permute-start(bf16[16384,128]{0,1:T(8,128)(2,1)} %get-tuple-element.10), channel_id=1, source_target_pairs={{0,4},{1,5},{2,6},{3,7},{4,0},{5,1},{6,2},{7,3},{8,12},{9,13},{10,... | collective-permute-start | bytes 12582920 | tf_op jit(solution)/shard_map/ppermute | solution.py:12
  619.4 179.8 %collective-permute-start.9 = (bf16[16384,128]{0,1:T(8,128)(2,1)S(1)}, bf16[16384,128]{0,1:T(8,128)(2,1)}, u32[]{:S(2)}, u32[]{:S(2)}) collective-permute-start(bf16[16384,128]{0,1:T(8,128)(2,1)S(1)} %fusion.15), channel_id=1, source_target_pairs={{0,8},{1,9},{2,10},{3,11},{4,12},{5,13},{6,14},{7,15},{8,0},{9,1},... | collective-permute-start | bytes 12582920 | tf_op jit(solution)/shard_map/ppermute | solution.py:12
  837.1 8.3 collective-permute-start.10
  845.5 1.4 collective-permute-start.11
Sparse Core Ops, SparseCore 0:
  370.2 89.0 all-reduce.2
  848.1 88.1 all-reduce.4
where the time goes:
time: 970 us; the launch traced here: 969 us
  waiting for transfers between devices  749 us (77%)
  matrix products  124 us (13%)
  other arithmetic  66.2 us (7%)
  between operations  14.3 us (1%)
    ppermute x12, waiting for transfers between devices, from_partner(): lax.ppermute(shard, axis, [(i, i ^ 1 << bit) for i in range(lax.axis_size...  575 us
    psum x2, waiting for transfers between devices, per_device(): gram_matrix = lax.psum(local_gram, 'row')  175 us
    dot_general x2, matrix products, per_device(): image = jnp.dot(tile_block, sketch, preferred_element_type=jnp.float32)  63.5 us
    dot_general x2, matrix products, per_device(): lax.dot_general(tile_block, panel, (((0,), (0,)), ((), ())), preferred_el...  57.2 us
    another operation x6, other arithmetic, orthonormal(): factor = jnp.linalg.cholesky(gram_matrix)  24.8 us
    another operation x4, other arithmetic, orthonormal(): lax.linalg.triangular_solve(factor, product, left_side=False, lower=True,...  20.9 us
  transfers between devices with their start and end apart: 14, of which 14 were waited for; matrix products, arithmetic and copies ran while one was open for 0% of the time, Pallas kernels for 0%

commit v1 on v0

--- a/solution.py
+++ b/solution.py
@@ -66,7 +66,8 @@
         local_gram = jnp.dot(
             image.T, image, precision=lax.Precision.HIGHEST, preferred_element_type=jnp.float32
         )
-        gram_matrix = lax.psum(local_gram, "row")
+        terms = lax.all_gather(local_gram, "row")
+        gram_matrix = jnp.sum(terms, axis=0)
         current = orthonormal(image, gram_matrix, rescale)
     return (current, sketch_block[None])
 

time: 970 us -> 873 us (0.900)
  waiting for transfers between devices: 749 us -> 647 us
    psum x2 -> x0, waiting for transfers between devices: 175 us -> none  [per_device(): gram_matrix = lax.psum(local_gram, 'row')]
    all_gather x0 -> x2, waiting for transfers between devices: none -> 74.5 us  [per_device(): terms = lax.all_gather(local_gram, 'row')]
where the time goes in v1:
time: 873 us; the launch traced here: 869 us
  waiting for transfers between devices  647 us (74%)
  matrix products  124 us (14%)
  other arithmetic  67.1 us (8%)
  between operations  14.3 us (2%)
  starting transfers between devices  12.6 us (1%)
    ppermute x12, waiting for transfers between devices, from_partner(): lax.ppermute(shard, axis, [(i, i ^ 1 << bit) for i in range(lax.axis_size...  573 us
    all_gather x2, waiting for transfers between devices, per_device(): terms = lax.all_gather(local_gram, 'row')  74.5 us
    dot_general x2, matrix products, per_device(): image = jnp.dot(tile_block, sketch, preferred_element_type=jnp.float32)  63.5 us
    dot_general x2, matrix products, per_device(): lax.dot_general(tile_block, panel, (((0,), (0,)), ((), ())), preferred_el...  57.2 us
    another operation x6, other arithmetic, orthonormal(): factor = jnp.linalg.cholesky(gram_matrix)  24.8 us
    another operation x4, other arithmetic, orthonormal(): lax.linalg.triangular_solve(factor, product, left_side=False, lower=True,...  20.9 us
  transfers between devices with their start and end apart: 14, of which 14 were waited for; matrix products, arithmetic and copies ran while one was open for 0% of the time, Pallas kernels for 0%

profile of v1, /device:TPU:8, one launch (start us, length us, event | category | flops | bytes accessed | tf_op | source)
XLA Modules:
  0.0 869.2 jit_solution(15765421749601292487)
XLA Ops:
  7.2 1.0 copy.17
  8.3 1.3 collective-permute-done
  9.7 1.6 collective-permute-start.1
  11.3 6.8 collective-permute-done.1
  18.2 28.6 %fusion.50 = (bf16[16384,128]{0,1:T(8,128)(2,1)}, f32[16384,128]{0,1:T(8,128)}) fusion(bf16[1,2048,16384]{2,1,0:T(8,128)(2,1)} %param.5, bf16[1024,128]{0,1:T(8,128)(2,1)S(1)} %maximum_select_fusion.4, bf16[1024,128]{0,1:T(8,128)(2,1)S(1)} %collective-permute-done.1, pred[]{:T(512)S(6)} %eq.22), kind=kOutput, calls=%fused_computation.70 | convolution fusion | flops 8594391040 | bytes 80216064 | tf_op jit(solution)/shard_map/dot_general | solution.py:46
  46.7 0.2 collective-permute-start.2
  47.0 91.8 %collective-permute-done.2 = bf16[16384,128]{0,1:T(8,128)(2,1)S(1)} collective-permute-done((bf16[16384,128]{0,1:T(8,128)(2,1)}, bf16[16384,128]{0,1:T(8,128)(2,1)S(1)}, u32[]{:S(2)}, u32[]{:S(2)}) %collective-permute-start.2) | collective-permute-done | bytes 4194336 | tf_op jit(solution)/shard_map/ppermute | solution.py:12
  138.8 5.7 fusion.14
  144.5 2.7 collective-permute-start.3
  147.1 178.2 %collective-permute-done.3 = bf16[16384,128]{0,1:T(8,128)(2,1)} collective-permute-done((bf16[16384,128]{0,1:T(8,128)(2,1)S(1)}, bf16[16384,128]{0,1:T(8,128)(2,1)}, u32[]{:S(2)}, u32[]{:S(2)}) %collective-permute-start.3) | collective-permute-done | bytes 4194336 | tf_op jit(solution)/shard_map/ppermute | solution.py:12
  325.3 33.8 %fusion.16 = f32[2048,128]{0,1:T(8,128)S(1)} fusion(bf16[1,2048,16384]{2,1,0:T(8,128)(2,1)} %param.5, bf16[16384,128]{0,1:T(8,128)(2,1)} %collective-permute-done.3, f32[16384,128]{0,1:T(8,128)} %get-tuple-element.11, bf16[16384,128]{0,1:T(8,128)(2,1)} %copy-done), kind=kOutput, calls=%fused_computation.16 | convolution fusion | flops 8600420352 | bytes 84934656 | tf_op jit(solution)/shard_map/dot_general | solution.py:57
  359.2 1.6 collective-permute-start.4
  360.8 6.7 collective-permute-done.4
  367.7 1.3 collective-permute-done.5
  369.0 1.0 fusion.46
  370.3 39.0 %all-gather.5.cloned.1.call-done = f32[2048,128]{1,0:T(8,128)} async-done(((f32[128,128]{1,0:T(8,128)}), f32[2048,128]{1,0:T(8,128)}) %all-gather.5.cloned.1.call-update) | async-done | bytes 1048592 | tf_op jit(solution)/shard_map/all_gather | solution.py:69
  409.3 1.3 reduce_sum.18
  410.7 11.7 %cholesky.44 = f32[128,128]{1,0:T(8,128)S(1)} custom-call(f32[128,128]{1,0:T(8,128)S(1)} %fusion.43), custom_call_target="Cholesky" | custom-call | tf_op jit(solution)/shard_map/jit(cholesky)/cholesky | solution.py:16
  422.4 0.6 compare_reduce_fusion.1
  423.1 0.7 fusion.38
  423.7 9.8 %custom-call.6 = f32[1,128,128]{1,2,0:T(8,128)S(1)} custom-call(f32[1,128,128]{2,1,0:T(8,128)S(1)} %fusion.38), custom_call_target="InvertDiagBlocksLowerTriangular" | custom-call | tf_op jit(solution)/shard_map/triangular_solve/custom-call.0 | solution.py:17
  433.6 0.4 fusion.24
  434.0 0.3 collective-permute-start.6
  434.3 1.1 collective-permute-done.6
  435.5 1.3 collective-permute-start.7
  436.8 7.3 collective-permute-done.7
  444.0 28.6 %fusion.51 = (bf16[16384,128]{0,1:T(8,128)(2,1)}, f32[16384,128]{0,1:T(8,128)}) fusion(bf16[1,2048,16384]{2,1,0:T(8,128)(2,1)} %param.5, bf16[1024,128]{0,1:T(8,128)(2,1)S(1)} %maximum_select_fusion.5, bf16[1024,128]{0,1:T(8,128)(2,1)S(1)} %collective-permute-done.7, pred[]{:T(512)S(6)} %eq.22), kind=kOutput, calls=%fused_computation.71 | convolution fusion | flops 8594391040 | bytes 80216064 | tf_op jit(solution)/shard_map/dot_general | solution.py:46
  472.6 1.5 collective-permute-start.8
  474.1 90.6 %collective-permute-done.8 = bf16[16384,128]{0,1:T(8,128)(2,1)S(1)} collective-permute-done((bf16[16384,128]{0,1:T(8,128)(2,1)}, bf16[16384,128]{0,1:T(8,128)(2,1)S(1)}, u32[]{:S(2)}, u32[]{:S(2)}) %collective-permute-start.8) | collective-permute-done | bytes 4194336 | tf_op jit(solution)/shard_map/ppermute | solution.py:12
  564.8 4.4 fusion.15
  569.2 2.3 collective-permute-start.9
  571.5 178.4 %collective-permute-done.9 = bf16[16384,128]{0,1:T(8,128)(2,1)} collective-permute-done((bf16[16384,128]{0,1:T(8,128)(2,1)S(1)}, bf16[16384,128]{0,1:T(8,128)(2,1)}, u32[]{:S(2)}, u32[]{:S(2)}) %collective-permute-start.9) | collective-permute-done | bytes 4194336 | tf_op jit(solution)/shard_map/ppermute | solution.py:12
  749.9 8.2 add_convert_fusion
  758.1 29.7 %fusion.19 = f32[2048,128]{0,1:T(8,128)S(1)} fusion(bf16[16384,128]{0,1:T(8,128)(2,1)} %add_convert_fusion, bf16[1,2048,16384]{2,1,0:T(8,128)(2,1)} %param.5), kind=kOutput, calls=%fused_computation.17 | convolution fusion | flops 8589934592 | bytes 72351744 | tf_op jit(solution)/shard_map/dot_general | solution.py:57
  787.9 0.6 collective-permute-start.10
  788.5 7.6 collective-permute-done.10
  796.3 1.3 collective-permute-done.11
  797.7 1.0 fusion.47
  798.7 1.3 constant_dynamic-slice_fusion
  800.0 1.3 copy.22
  801.4 35.6 %all-gather.7.cloned.1.call-done = f32[2048,128]{1,0:T(8,128)} async-done(((f32[128,128]{1,0:T(8,128)}), f32[2048,128]{1,0:T(8,128)}) %all-gather.7.cloned.1.call-update) | async-done | bytes 1048592 | tf_op jit(solution)/shard_map/all_gather | solution.py:69
  836.9 1.3 reduce_sum.19
  838.3 11.7 %cholesky.55 = f32[128,128]{1,0:T(8,128)S(1)} custom-call(f32[128,128]{1,0:T(8,128)S(1)} %fusion.41), custom_call_target="Cholesky" | custom-call | tf_op jit(solution)/shard_map/jit(cholesky)/cholesky | solution.py:16
  850.1 0.6 compare_reduce_fusion
  850.7 0.7 fusion.39
  851.4 9.8 %custom-call.7 = f32[1,128,128]{1,2,0:T(8,128)S(1)} custom-call(f32[1,128,128]{2,1,0:T(8,128)S(1)} %fusion.39), custom_call_target="InvertDiagBlocksLowerTriangular" | custom-call | tf_op jit(solution)/shard_map/triangular_solve/custom-call.0 | solution.py:17
  861.2 0.4 fusion.25
  861.6 0.8 copy.23
  (23 shorter events, 1.3 us)
Async XLA Ops:
  7.2 402.1 %all-gather.5.cloned.1.call-start = ((), (), s32[]{:S(2)}) async-start(), calls=%async_computation | async-start | bytes 1114112 | tf_op jit(solution)/shard_map/all_gather | solution.py:69
  8.2 1.4 collective-permute-start
  9.7 8.4 collective-permute-start.1
  46.7 92.0 %collective-permute-start.2 = (bf16[16384,128]{0,1:T(8,128)(2,1)}, bf16[16384,128]{0,1:T(8,128)(2,1)S(1)}, u32[]{:S(2)}, u32[]{:S(2)}) collective-permute-start(bf16[16384,128]{0,1:T(8,128)(2,1)} %get-tuple-element.10), channel_id=1, source_target_pairs={{0,4},{1,5},{2,6},{3,7},{4,0},{5,1},{6,2},{7,3},{8,12},{9,13},{10,... | collective-permute-start | bytes 12582920 | tf_op jit(solution)/shard_map/ppermute | solution.py:12
  138.8 5.7 copy-start
  144.5 180.8 %collective-permute-start.3 = (bf16[16384,128]{0,1:T(8,128)(2,1)S(1)}, bf16[16384,128]{0,1:T(8,128)(2,1)}, u32[]{:S(2)}, u32[]{:S(2)}) collective-permute-start(bf16[16384,128]{0,1:T(8,128)(2,1)S(1)} %fusion.14), channel_id=1, source_target_pairs={{0,8},{1,9},{2,10},{3,11},{4,12},{5,13},{6,14},{7,15},{8,0},{9,1},... | collective-permute-start | bytes 12582920 | tf_op jit(solution)/shard_map/ppermute | solution.py:12
  359.2 8.3 collective-permute-start.4
  367.6 1.4 collective-permute-start.5
  370.1 466.8 %all-gather.7.cloned.1.call-start = ((), (), s32[]{:S(2)}) async-start(), calls=%async_computation.1 | async-start | bytes 1114112 | tf_op jit(solution)/shard_map/all_gather | solution.py:69
  434.0 1.4 collective-permute-start.6
  435.5 8.5 collective-permute-start.7
  472.6 92.1 %collective-permute-start.8 = (bf16[16384,128]{0,1:T(8,128)(2,1)}, bf16[16384,128]{0,1:T(8,128)(2,1)S(1)}, u32[]{:S(2)}, u32[]{:S(2)}) collective-permute-start(bf16[16384,128]{0,1:T(8,128)(2,1)} %get-tuple-element.12), channel_id=1, source_target_pairs={{0,4},{1,5},{2,6},{3,7},{4,0},{5,1},{6,2},{7,3},{8,12},{9,13},{10,... | collective-permute-start | bytes 12582920 | tf_op jit(solution)/shard_map/ppermute | solution.py:12
  569.2 180.7 %collective-permute-start.9 = (bf16[16384,128]{0,1:T(8,128)(2,1)S(1)}, bf16[16384,128]{0,1:T(8,128)(2,1)}, u32[]{:S(2)}, u32[]{:S(2)}) collective-permute-start(bf16[16384,128]{0,1:T(8,128)(2,1)S(1)} %fusion.15), channel_id=1, source_target_pairs={{0,8},{1,9},{2,10},{3,11},{4,12},{5,13},{6,14},{7,15},{8,0},{9,1},... | collective-permute-start | bytes 12582920 | tf_op jit(solution)/shard_map/ppermute | solution.py:12
  787.9 8.3 collective-permute-start.10
  796.3 1.4 collective-permute-start.11
Sparse Core Ops, SparseCore 0:
  370.2 39.0 all-gather.4
  798.8 38.0 all-gather.6
